TPU v7x, 32 devices: a whole 2x2x4 slice. The times are simulated.
32 devices in a mesh: head: 2 (over core), blk: 16 (over z, y, x).
Axes of the slice: x: 2, y: 2, z: 4, core: 2. Of those that a mesh axis runs over, the one named last changes fastest.
Arguments:
- queries: bfloat16 [4096, 1024], P('blk', 'head'), may hold values from -5.5 to 5.5
- new_keys: bfloat16 [4096, 1024], P('blk', 'head'), may hold values from -5.5 to 5.5
- new_values: bfloat16 [4096, 1024], P('blk', 'head'), may hold values from -6 to 6
- sink_keys: bfloat16 [16, 4, 1024], P('blk', None, 'head'), may hold values from -16 to 16
- sink_values: bfloat16 [16, 4, 1024], P('blk', None, 'head'), may hold values from -6 to 6
- pool_keys: bfloat16 [16, 9, 512, 1024], P('blk', None, None, 'head'), may hold values from -6 to 6
- pool_values: bfloat16 [16, 9, 512, 1024], P('blk', None, None, 'head'), may hold values from -6 to 6
- block_ids: int32 [16, 9], replicated, may hold values from 1 to 64, as said below
- cache_lengths: int32 [16], replicated, may hold values from 4608 to 32768, as said below
- cross_keys: bfloat16 [16, 128, 1024], P('blk', None, 'head'), may hold values from -6 to 6
- cross_values: bfloat16 [16, 128, 1024], P('blk', None, 'head'), may hold values from -6 to 6
- enc_lengths: int32 [16], P('blk'), may hold values from 32 to 128
- hidden: bfloat16 [4096, 1024], P('blk', 'head'), may hold values from -6 to 6
- w_out_t: bfloat16 [1024, 1024], P(None, 'head'), may hold values from -0.1875 to 0.1875
- gain_self: float32 [1024], replicated, may hold values from 0.25 to 1.75
- bias_self: float32 [1024], replicated, may hold values from -0.5 to 0.5
- w_cross_q: bfloat16 [1024, 1024], P(None, 'head'), may hold values from -0.1875 to 0.1875
- w_cross_out_t: bfloat16 [1024, 1024], P(None, 'head'), may hold values from -0.1875 to 0.1875
- gain_cross: float32 [1024], replicated, may hold values from 0.25 to 1.75
- bias_cross: float32 [1024], replicated, may hold values from -0.5 to 0.5
Outputs:
- layer_out: bfloat16 [4096, 1024], P('blk', 'head')
Inputs may be any that keep to these rules, and one draw needn't show every extreme that they name: `cache_lengths`: one request has exactly 32768 cached tokens and another exactly 4608. `block_ids`: entry [g, s] belongs to request (g - s - 1) mod 16; the 9 entries of request r hold the consecutive block numbers from (cache_lengths[r] - 4095) // 512 on, each once, in an order drawn from the seed.
All inputs are finite; a program needn't handle non-finite values.
Results may differ from a plain program's by a relative error of at most 0.02.
Values may be sent and summed in bfloat16 or wider, within the bound.
A program may use at most 192 MiB of HBM per device.

v0:
```python
import functools

import jax
import jax.numpy as jnp
from jax import lax
from jax.experimental import pallas as pl
from jax.experimental.pallas import tpu as pltpu
from jax.sharding import PartitionSpec as P

HD = 64
WINDOW = 4096
GROUP = 4
LOG2E = 1.4426950408889634

masked_score = -1e30
norm_eps = 1e-05


def split_terms(stats):
    high = stats.astype(jnp.bfloat16).astype(jnp.float32)
    rest = stats - high
    middle = rest.astype(jnp.bfloat16).astype(jnp.float32)
    low = rest - middle
    return jnp.concatenate([high, middle, low, jnp.zeros_like(high)], axis=0).astype(jnp.bfloat16)


def attend_pairs(q, k_ref, v_ref, bias):
    rows, width = q.shape
    lane = lax.broadcasted_iota(jnp.int32, (rows, 2 * HD), 1)
    first = lane < HD
    both = jnp.concatenate([bias, bias], axis=1)
    outs, stats = [], []
    for pair in range(width // (2 * HD)):
        cols = slice(pair * 2 * HD, (pair + 1) * 2 * HD)
        part = q[:, cols]
        zero = jnp.zeros_like(part)
        q2 = jnp.concatenate([jnp.where(first, part, zero), jnp.where(first, zero, part)], axis=0)
        scores = lax.dot_general(
            k_ref[:, cols], q2, (((1,), (1,)), ((), ())), preferred_element_type=jnp.float32
        )
        scores = scores * (HD ** (-0.5) * LOG2E) + both
        top = jnp.max(scores, axis=0, keepdims=True)
        weights = jnp.exp2(scores - top)
        total = jnp.sum(weights, axis=0, keepdims=True)
        summed = lax.dot_general(
            v_ref[:, cols],
            weights.astype(jnp.bfloat16),
            (((0,), (0,)), ((), ())),
            preferred_element_type=jnp.float32,
        )
        inverse = 1.0 / total
        lse = top + jnp.log2(total)
        outs += [summed[:HD, :rows] * inverse[:, :rows], summed[HD:, rows:] * inverse[:, rows:]]
        stats += [lse[:, :rows], lse[:, rows:]]
    return outs, stats


def store_part(out_ref, outs, stats):
    for i, out in enumerate(outs):
        out_ref[i * HD : (i + 1) * HD, :] = out.astype(jnp.bfloat16)
    width = len(outs) * HD
    out_ref[width : width + 4 * len(outs), :] = split_terms(jnp.concatenate(stats, axis=0))


def merge(refs, flags):
    heads = refs[0].shape[0] // (HD + 4)
    width = heads * HD
    lses = []
    for ref, flag in zip(refs, flags):
        terms = ref[width:, :].astype(jnp.float32)
        lse = terms[:heads] + terms[heads : 2 * heads] + terms[2 * heads : 3 * heads]
        lses.append(lse if flag is True else jnp.where(flag, lse, 2.0 * masked_score))
    top = functools.reduce(jnp.maximum, lses)
    weights = [jnp.exp2(lse - top) for lse in lses]
    total = sum(weights)
    inverse = 1.0 / total
    weights = [w * inverse for w in weights]
    lse = top + jnp.log2(total)
    outs, stats = [], []
    for head in range(heads):
        rows = slice(head * HD, (head + 1) * HD)
        outs.append(
            sum(ref[rows, :].astype(jnp.float32) * w[head : head + 1] for ref, w in zip(refs, weights))
        )
        stats.append(lse[head : head + 1])
    return outs, stats


def layer_kernel(
    count,
    slots,
    sinks,
    block_ids,
    cache_lengths,
    enc_lengths,
    queries,
    new_keys,
    new_values,
    sink_keys,
    sink_values,
    pool_keys,
    pool_values,
    cross_keys,
    cross_values,
    hidden,
    w_out,
    gain_self,
    bias_self,
    w_query,
    w_cross,
    gain_cross,
    bias_cross,
    out,
    k_buf,
    v_buf,
    k_own,
    v_own,
    q_far,
    q_near,
    part,
    near,
    merged,
    far,
    own_part,
    own_merged,
    w_mine,
    w_theirs,
    w_theirs_query,
    cross_mine,
    cross_theirs,
    hidden_theirs,
    turned,
    turned_theirs,
    out_send,
    out_theirs,
    kv_sem,
    own_sem,
    qf_send,
    qf_recv,
    qn_send,
    qn_recv,
    pn_send,
    pn_recv,
    pf_send,
    pf_recv,
    sib_send,
    sib_recv,
):
    device = lax.axis_index("blk")
    head = lax.axis_index("head")
    lane = lax.rem(device, GROUP)
    base = device - lane
    rows, width = queries.shape
    half = rows // 2
    mesh_id = pl.DeviceIdType.MESH

    def at_far(distance):
        return (head, lax.rem(device + count + GROUP * distance, count))

    def at_near(shift):
        return (head, base + lax.rem(lane + GROUP + shift, GROUP))

    sibling = (1 - head, device)

    local = [
        pltpu.make_async_copy(w_out, w_mine.at[0], own_sem.at[0]),
        pltpu.make_async_copy(w_cross, w_mine.at[1], own_sem.at[1]),
        pltpu.make_async_copy(cross_keys.at[0], cross_mine.at[0], own_sem.at[2]),
        pltpu.make_async_copy(cross_values.at[0], cross_mine.at[1], own_sem.at[3]),
    ]
    order = [4, 1, 2, 3, 5, 6, 7, 8, 9]

    def pool_copies(s):
        return (
            pltpu.make_async_copy(pool_keys.at[0, s - 1], k_buf.at[s - 1], kv_sem.at[0, s - 1]),
            pltpu.make_async_copy(pool_values.at[0, s - 1], v_buf.at[s - 1], kv_sem.at[1, s - 1]),
        )

    for s in order:
        for copy in pool_copies(s):
            copy.start()
    for copy in local:
        copy.start()

    barrier = pltpu.get_barrier_semaphore()
    partners = [at_far(d) for d in (1, 2, 3, -1, -2, -3)] + [at_near(d) for d in (1, 2, 3)] + [sibling]
    for partner in partners:
        pl.semaphore_signal(barrier, inc=1, device_id=partner, device_id_type=mesh_id)

    k_own[:rows, :] = new_keys[...]
    v_own[:rows, :] = new_values[...]
    k_own[rows : rows + 16, :] = sink_keys[...]
    v_own[rows : rows + 16, :] = sink_values[...]
    pad = k_own.shape[0] - rows - 16
    k_own[rows + 16 :, :] = jnp.zeros((pad, width), jnp.bfloat16)
    v_own[rows + 16 :, :] = jnp.zeros((pad, width), jnp.bfloat16)

    pl.semaphore_wait(barrier, len(partners))

    def remote(source, target, send, recv, device_id):
        return pltpu.make_async_remote_copy(
            src_ref=source,
            dst_ref=target,
            send_sem=send,
            recv_sem=recv,
            device_id=device_id,
            device_id_type=mesh_id,
        )

    def query_far(distance):
        i = distance - 1
        return remote(queries, q_far.at[i], qf_send.at[i], qf_recv.at[i], at_far(distance))

    def query_near(s, source):
        return remote(source, q_near.at[s - 1], qn_send.at[s - 1], qn_recv.at[s - 1], at_near(s % GROUP))

    def part_near(s):
        shift = lax.rem(s, GROUP)
        target = (head, base + lax.rem(lane + GROUP - shift, GROUP))
        return remote(part.at[s - 1], near.at[s - 1], pn_send.at[s - 1], pn_recv.at[s - 1], target)

    def part_far(distance, source):
        i = distance - 1
        return remote(source, far.at[i], pf_send.at[i], pf_recv.at[i], at_far(-distance))

    query_far(2).start()
    query_far(1).start()
    last = lane == GROUP - 1

    @pl.when(last)
    def _():
        query_far(3).start()

    @pl.when(jnp.logical_not(last))
    def _():
        far[2] = jnp.zeros(far.shape[1:], far.dtype)

    moves = [s for s in range(1, slots + 1) if s % GROUP]

    def forward(distance):
        source = queries if distance == 0 else q_far.at[distance - 1]
        for s in moves:
            if s // GROUP == distance or s // GROUP + 1 == distance:
                wraps = lane + s % GROUP >= GROUP
                here = wraps if s // GROUP + 1 == distance else jnp.logical_not(wraps)

                @pl.when(here)
                def _():
                    query_near(s, source).start()

    forward(0)
    other_rows = pl.ds(pl.multiple_of((1 - head) * half, half), half)
    to_sibling = [
        (hidden.at[other_rows, :], hidden_theirs),
        (w_out, w_theirs.at[0]),
        (cross_keys.at[0], cross_theirs.at[0]),
        (cross_values.at[0], cross_theirs.at[1]),
        (w_query, w_theirs_query),
        (w_cross, w_theirs.at[1]),
    ]
    shared = [
        remote(a, b, sib_send.at[i], sib_recv.at[i], sibling) for i, (a, b) in enumerate(to_sibling)
    ]
    for copy in shared:
        copy.start()

    index = lax.broadcasted_iota(jnp.int32, (k_own.shape[0], rows), 0)
    token = lax.broadcasted_iota(jnp.int32, (k_own.shape[0], rows), 1)
    visible = (index <= token) | ((index >= rows) & (index < rows + sinks))
    bias = jnp.where(visible, 0.0, masked_score)
    store_part(own_part, *attend_pairs(queries[...], k_own, v_own, bias))

    def compute(s, q_ref, target):
        for copy in pool_copies(s):
            copy.wait()
        asker = lax.rem(device + count - s, count)
        keys = k_buf.shape[1]
        start = block_ids[device, s - 1] * keys - cache_lengths[asker]
        relative = start + lax.broadcasted_iota(jnp.int32, (keys, rows), 0)
        token = lax.broadcasted_iota(jnp.int32, (keys, rows), 1)
        visible = (relative > token - WINDOW) & (relative < 0)
        bias = jnp.where(visible, 0.0, masked_score)
        store_part(target, *attend_pairs(q_ref[...], k_buf.at[s - 1], v_buf.at[s - 1], bias))

    def moved_step(s, carry=0):
        remote(
            queries, q_near.at[s - 1], qn_send.at[s - 1], qn_recv.at[s - 1], sibling
        ).wait_recv()
        compute(s, q_near.at[s - 1], part.at[s - 1])
        part_near(s).start()
        return carry

    def wait_near(s, condition):
        @pl.when(condition)
        def _():
            part_near(s).wait_recv()

    query_far(1).wait_recv()
    forward(1)
    compute(4, q_far.at[0], near.at[3])
    query_far(2).wait_recv()
    forward(2)
    lax.fori_loop(1, 4, moved_step, 0)

    @pl.when(last)
    def _():
        query_far(3).wait_recv()

    forward(3)
    lax.fori_loop(5, 8, moved_step, 0)
    compute(8, q_far.at[1], near.at[7])

    def merge_group(distance):
        refs, flags = [], []
        for j in range(GROUP):
            s = GROUP * distance - lane + j
            inside = s <= slots
            wait_near(s, jnp.logical_and(inside, lane != j))
            refs.append(near.at[jnp.minimum(s, slots) - 1])
            flags.append(True if distance == 1 else inside)
        store_part(merged.at[distance - 1], *merge(refs, flags))
        part_far(distance, merged.at[distance - 1]).start()

    moved_step(9)
    merge_group(1)
    merge_group(2)

    @pl.when(last)
    def _():
        part_near(9).wait_recv()
        part_far(3, near.at[8]).start()

    refs, flags = [own_part], [True]
    for s in range(1, GROUP):
        inside = lane + s < GROUP
        wait_near(s, inside)
        refs.append(near.at[s - 1])
        flags.append(inside)
    store_part(own_merged, *merge(refs, flags))
    part_far(1, merged.at[0]).wait_recv()
    part_far(2, merged.at[1]).wait_recv()

    @pl.when(last)
    def _():
        part_far(3, near.at[8]).wait_recv()

    outs, _ = merge([own_merged] + [far.at[i] for i in range(3)], [True, True, True, last])

    for i in range(2):
        cut = slice(i * half, (i + 1) * half)
        turned[i] = jnp.concatenate([o[:, cut] for o in outs], axis=0).T.astype(jnp.bfloat16)
    send_turned = remote(turned.at[1 - head], turned_theirs, sib_send.at[6], sib_recv.at[6], sibling)
    send_turned.start()

    for copy in local:
        copy.wait()
    for copy in shared:
        copy.wait()

    def project_back(rows_in, weight):
        return lax.dot_general(
            rows_in, weight, (((1,), (1,)), ((), ())), preferred_element_type=jnp.float32
        )

    def ordered(mine, theirs):
        is_first = head == 0
        return jnp.concatenate(
            [jnp.where(is_first, mine, theirs), jnp.where(is_first, theirs, mine)], axis=1
        )

    def full_norm(pre_norm, gain, bias_row):
        row_mean = jnp.mean(pre_norm, axis=-1, keepdims=True)
        centered = pre_norm - row_mean
        row_var = jnp.mean(centered * centered, axis=-1, keepdims=True)
        return centered * lax.rsqrt(row_var + norm_eps) * gain[...] + bias_row[...]

    own_rows = pl.ds(pl.multiple_of(head * half, half), half)
    residual = ordered(
        hidden[own_rows, :].astype(jnp.float32), hidden_theirs[...].astype(jnp.float32)
    )
    pre = residual + project_back(turned[head], w_mine[0])
    send_turned.wait()
    pre = pre + project_back(turned_theirs[...], w_theirs[0])
    normed = full_norm(pre, gain_self, bias_self).astype(jnp.bfloat16)

    enc = cross_mine.shape[1]
    seen = lax.broadcasted_iota(jnp.int32, (enc, half), 0) < enc_lengths[0]
    enc_bias = jnp.where(seen, 0.0, masked_score)
    second = normed.astype(jnp.float32)
    for wq, kv, w_back in (
        (w_query, cross_mine, w_mine.at[1]),
        (w_theirs_query, cross_theirs, w_theirs.at[1]),
    ):
        cross_query = jnp.dot(normed, wq[...], preferred_element_type=jnp.float32).astype(jnp.bfloat16)
        context, _ = attend_pairs(cross_query, kv.at[0], kv.at[1], enc_bias)
        context = jnp.concatenate(context, axis=0).T.astype(jnp.bfloat16)
        second = second + project_back(context, w_back[...])
    result = full_norm(second, gain_cross, bias_cross)
    left, right = result[:, :width], result[:, width:]
    is_first = head == 0
    out_send[...] = jnp.where(is_first, right, left).astype(jnp.bfloat16)
    send_out = remote(out_send, out_theirs, sib_send.at[7], sib_recv.at[7], sibling)
    send_out.start()
    out[own_rows, :] = jnp.where(is_first, left, right).astype(jnp.bfloat16)

    for s in moves:
        query_near(s, queries).wait_send()
        part_near(s).wait_send()
    for distance in (1, 2):
        query_far(distance).wait_send()
        part_far(distance, merged.at[distance - 1]).wait_send()

    @pl.when(last)
    def _():
        query_far(3).wait_send()
        part_far(3, near.at[8]).wait_send()

    send_out.wait()
    out[other_rows, :] = out_theirs[...]


def per_device(
    queries,
    new_keys,
    new_values,
    sink_keys,
    sink_values,
    pool_keys,
    pool_values,
    block_ids,
    cache_lengths,
    cross_keys,
    cross_values,
    enc_lengths,
    hidden,
    w_out_t,
    gain_self,
    bias_self,
    w_cross_q,
    w_cross_out_t,
    gain_cross,
    bias_cross,
):
    count = lax.axis_size("blk")
    rows, width = queries.shape
    slots, keys = pool_keys.shape[1:3]
    sinks = sink_keys.shape[1]
    enc = cross_keys.shape[1]
    full = w_out_t.shape[0]
    half = rows // 2
    packed = width + 4 * (width // HD)
    pad = ((0, 16 - sinks), (0, 0))
    whole = pl.BlockSpec(memory_space=pltpu.VMEM)
    smem = pl.BlockSpec(memory_space=pltpu.SMEM)
    hbm = pl.BlockSpec(memory_space=pl.ANY)

    def buf(*shape):
        return pltpu.VMEM(shape, jnp.bfloat16)

    dma = pltpu.SemaphoreType.DMA
    return pl.pallas_call(
        functools.partial(layer_kernel, count, slots, sinks),
        out_shape=jax.ShapeDtypeStruct((rows, width), jnp.bfloat16),
        in_specs=[smem] * 3
        + [whole] * 5
        + [hbm] * 4
        + [whole, hbm, whole, whole, whole, hbm, whole, whole],
        out_specs=whole,
        scratch_shapes=[
            buf(slots, keys, width),
            buf(slots, keys, width),
            buf(rows + 128, width),
            buf(rows + 128, width),
            buf(3, rows, width),
            buf(slots, rows, width),
            buf(slots, packed, rows),
            buf(slots, packed, rows),
            buf(2, packed, rows),
            buf(3, packed, rows),
            buf(packed, rows),
            buf(packed, rows),
            buf(2, full, width),
            buf(2, full, width),
            buf(full, width),
            buf(2, enc, width),
            buf(2, enc, width),
            buf(half, width),
            buf(2, half, width),
            buf(half, width),
            buf(half, width),
            buf(half, width),
            dma((2, slots)),
            dma((4,)),
            dma((3,)),
            dma((3,)),
            dma((slots,)),
            dma((slots,)),
            dma((slots,)),
            dma((slots,)),
            dma((3,)),
            dma((3,)),
            dma((8,)),
            dma((8,)),
        ],
        compiler_params=pltpu.CompilerParams(
            collective_id=0, has_side_effects=True, vmem_limit_bytes=52 * 1024 * 1024
        ),
        cost_estimate=pl.CostEstimate(
            flops=4 * rows * keys * width * slots,
            bytes_accessed=4 * keys * width * slots,
            transcendentals=rows * keys * slots * (width // HD),
        ),
    )(
        block_ids,
        cache_lengths,
        enc_lengths,
        queries,
        new_keys,
        new_values,
        jnp.pad(sink_keys[0], pad),
        jnp.pad(sink_values[0], pad),
        pool_keys,
        pool_values,
        cross_keys,
        cross_values,
        hidden,
        w_out_t,
        gain_self.reshape(1, -1),
        bias_self.reshape(1, -1),
        w_cross_q,
        w_cross_out_t,
        gain_cross.reshape(1, -1),
        bias_cross.reshape(1, -1),
    )


def solution(mesh):
    placed = (
        P("blk", "head"),
        P("blk", "head"),
        P("blk", "head"),
        P("blk", None, "head"),
        P("blk", None, "head"),
        P("blk", None, None, "head"),
        P("blk", None, None, "head"),
        P(),
        P(),
        P("blk", None, "head"),
        P("blk", None, "head"),
        P("blk"),
        P("blk", "head"),
        P(None, "head"),
        P(),
        P(),
        P(None, "head"),
        P(None, "head"),
        P(),
        P(),
    )
    return jax.shard_map(
        per_device, mesh=mesh, in_specs=placed, out_specs=P("blk", "head"), check_vma=False
    )
```

profile of v0, /device:TPU:0, one launch (start us, length us, event | category | flops | bytes accessed | tf_op | source)
XLA Modules:
  0.0 116.3 jit_solution(1437075676962761580)
XLA Ops:
  0.7 0.7 pad.7.sink_keys
  1.3 0.7 pad.8.sink_values
  2.0 0.0 copy-start
  2.0 0.9 copy-done
  3.0 0.0 copy-start.1
  3.0 0.9 copy-done.1
  3.9 0.0 copy-start.2
  3.9 0.9 copy-done.2
  4.9 0.0 copy-start.3
  4.9 0.9 copy-done.3
  5.8 0.0 copy-start.4
  5.8 0.9 copy-done.4
  6.7 0.0 copy-start.5
  6.7 0.9 copy-done.5
  7.7 0.0 copy-start.6
  7.7 0.7 copy-done.6
  8.3 0.0 copy-start.7
  8.4 0.7 copy-done.7
  9.0 0.0 copy-start.8
  9.0 0.7 copy-done.8
  9.7 0.0 copy-start.9
  9.7 0.7 copy-done.9
  10.4 0.0 copy-start.10
  10.4 0.7 copy-done.10
  11.1 0.0 copy-start.11
  11.1 0.7 copy-done.11
  11.8 103.8 %shard_map.190 = bf16[256,512]{1,0:T(8,128)(2,1)S(1)} custom-call(s32[16,9]{1,0:T(8,128)S(1)} %copy-done.6, s32[16]{0:T(128)S(1)} %copy-done.11, s32[1]{0:T(128)S(6)} %copy.22.enc_lengths, bf16[256,512]{1,0:T(8,128)(2,1)S(1)} %copy-done, bf16[256,512]{1,0:T(8,128)(2,1)S(1)} %copy-done.1, bf16[256,512]{1,0:T(8,128)(2,1)S(1)} %copy-done.2, ...), custom_call_target="tpu_custom_call" | custom-call | flops 2415919104 | bytes 9437184 | tf_op jit(solution)/shard_map/pallas_call | solution.py:461
  115.6 0.7 copy.23
Async XLA Ops:
  2.0 0.9 copy-start
  3.0 0.9 copy-start.1
  3.9 0.9 copy-start.2
  4.9 0.9 copy-start.3
  5.8 0.9 copy-start.4
  6.7 0.9 copy-start.5
  7.7 0.7 copy-start.6
  8.3 0.7 copy-start.7
  9.0 0.7 copy-start.8
  9.7 0.7 copy-start.9
  10.4 0.7 copy-start.10
  11.1 0.7 copy-start.11
where the time goes:
time: 117 us; the launch traced here: 116 us
  Pallas kernels  104 us (89%)
  local copies, waits for them, and re-layouts  11.8 us (10%)
    pallas_call x1, Pallas kernels, per_device(): pl.pallas_call(functools.partial(layer_kernel, count, slots, sinks), out_...  104 us
    unnamed x25, local copies, waits for them, and re-layouts  10.4 us

commit v1 on v0

--- a/solution.py
+++ b/solution.py
@@ -96,8 +96,7 @@
     queries,
     new_keys,
     new_values,
-    sink_keys,
-    sink_values,
+    sink_pair,
     pool_keys,
     pool_values,
     cross_keys,
@@ -115,6 +114,10 @@
     v_buf,
     k_own,
     v_own,
+    q_own,
+    hidden_mine,
+    w_query_mine,
+    norms,
     q_far,
     q_near,
     part,
@@ -161,12 +164,32 @@
         return (head, base + lax.rem(lane + GROUP + shift, GROUP))
 
     sibling = (1 - head, device)
+    own_rows = pl.ds(pl.multiple_of(head * half, half), half)
+    other_rows = pl.ds(pl.multiple_of((1 - head) * half, half), half)
+
+    barrier = pltpu.get_barrier_semaphore()
+    partners = [at_far(d) for d in (1, 2, 3, -1, -2, -3)] + [at_near(d) for d in (1, 2, 3)] + [sibling]
+    for partner in partners:
+        pl.semaphore_signal(barrier, inc=1, device_id=partner, device_id_type=mesh_id)
 
     local = [
         pltpu.make_async_copy(w_out, w_mine.at[0], own_sem.at[0]),
         pltpu.make_async_copy(w_cross, w_mine.at[1], own_sem.at[1]),
         pltpu.make_async_copy(cross_keys.at[0], cross_mine.at[0], own_sem.at[2]),
         pltpu.make_async_copy(cross_values.at[0], cross_mine.at[1], own_sem.at[3]),
+        pltpu.make_async_copy(w_query, w_query_mine, own_sem.at[4]),
+        pltpu.make_async_copy(gain_self, norms.at[0], own_sem.at[5]),
+        pltpu.make_async_copy(bias_self, norms.at[1], own_sem.at[6]),
+        pltpu.make_async_copy(gain_cross, norms.at[2], own_sem.at[7]),
+        pltpu.make_async_copy(bias_cross, norms.at[3], own_sem.at[8]),
+        pltpu.make_async_copy(hidden.at[own_rows, :], hidden_mine, own_sem.at[9]),
+    ]
+    early = [
+        pltpu.make_async_copy(queries, q_own, own_sem.at[10]),
+        pltpu.make_async_copy(new_keys, k_own.at[pl.ds(0, rows), :], own_sem.at[11]),
+        pltpu.make_async_copy(new_values, v_own.at[pl.ds(0, rows), :], own_sem.at[12]),
+        pltpu.make_async_copy(sink_pair.at[0], k_own.at[pl.ds(rows, 16), :], own_sem.at[13]),
+        pltpu.make_async_copy(sink_pair.at[1], v_own.at[pl.ds(rows, 16), :], own_sem.at[14]),
     ]
     order = [4, 1, 2, 3, 5, 6, 7, 8, 9]
 
@@ -176,21 +199,9 @@
             pltpu.make_async_copy(pool_values.at[0, s - 1], v_buf.at[s - 1], kv_sem.at[1, s - 1]),
         )
 
-    for s in order:
-        for copy in pool_copies(s):
-            copy.start()
-    for copy in local:
+    for copy in early:
         copy.start()
 
-    barrier = pltpu.get_barrier_semaphore()
-    partners = [at_far(d) for d in (1, 2, 3, -1, -2, -3)] + [at_near(d) for d in (1, 2, 3)] + [sibling]
-    for partner in partners:
-        pl.semaphore_signal(barrier, inc=1, device_id=partner, device_id_type=mesh_id)
-
-    k_own[:rows, :] = new_keys[...]
-    v_own[:rows, :] = new_values[...]
-    k_own[rows : rows + 16, :] = sink_keys[...]
-    v_own[rows : rows + 16, :] = sink_values[...]
     pad = k_own.shape[0] - rows - 16
     k_own[rows + 16 :, :] = jnp.zeros((pad, width), jnp.bfloat16)
     v_own[rows + 16 :, :] = jnp.zeros((pad, width), jnp.bfloat16)
@@ -249,7 +260,11 @@
                     query_near(s, source).start()
 
     forward(0)
-    other_rows = pl.ds(pl.multiple_of((1 - head) * half, half), half)
+    for s in order:
+        for copy in pool_copies(s):
+            copy.start()
+    for copy in local:
+        copy.start()
     to_sibling = [
         (hidden.at[other_rows, :], hidden_theirs),
         (w_out, w_theirs.at[0]),
@@ -261,14 +276,13 @@
     shared = [
         remote(a, b, sib_send.at[i], sib_recv.at[i], sibling) for i, (a, b) in enumerate(to_sibling)
     ]
-    for copy in shared:
-        copy.start()
-
     index = lax.broadcasted_iota(jnp.int32, (k_own.shape[0], rows), 0)
     token = lax.broadcasted_iota(jnp.int32, (k_own.shape[0], rows), 1)
+    for copy in early:
+        copy.wait()
     visible = (index <= token) | ((index >= rows) & (index < rows + sinks))
     bias = jnp.where(visible, 0.0, masked_score)
-    store_part(own_part, *attend_pairs(queries[...], k_own, v_own, bias))
+    store_part(own_part, *attend_pairs(q_own[...], k_own, v_own, bias))
 
     def compute(s, q_ref, target):
         for copy in pool_copies(s):
@@ -300,6 +314,8 @@
     compute(4, q_far.at[0], near.at[3])
     query_far(2).wait_recv()
     forward(2)
+    for copy in shared:
+        copy.start()
     lax.fori_loop(1, 4, moved_step, 0)
 
     @pl.when(last)
@@ -321,8 +337,8 @@
         store_part(merged.at[distance - 1], *merge(refs, flags))
         part_far(distance, merged.at[distance - 1]).start()
 
+    merge_group(1)
     moved_step(9)
-    merge_group(1)
     merge_group(2)
 
     @pl.when(last)
@@ -374,28 +390,27 @@
         row_var = jnp.mean(centered * centered, axis=-1, keepdims=True)
         return centered * lax.rsqrt(row_var + norm_eps) * gain[...] + bias_row[...]
 
-    own_rows = pl.ds(pl.multiple_of(head * half, half), half)
     residual = ordered(
-        hidden[own_rows, :].astype(jnp.float32), hidden_theirs[...].astype(jnp.float32)
+        hidden_mine[...].astype(jnp.float32), hidden_theirs[...].astype(jnp.float32)
     )
     pre = residual + project_back(turned[head], w_mine[0])
     send_turned.wait()
     pre = pre + project_back(turned_theirs[...], w_theirs[0])
-    normed = full_norm(pre, gain_self, bias_self).astype(jnp.bfloat16)
+    normed = full_norm(pre, norms.at[0], norms.at[1]).astype(jnp.bfloat16)
 
     enc = cross_mine.shape[1]
     seen = lax.broadcasted_iota(jnp.int32, (enc, half), 0) < enc_lengths[0]
     enc_bias = jnp.where(seen, 0.0, masked_score)
     second = normed.astype(jnp.float32)
     for wq, kv, w_back in (
-        (w_query, cross_mine, w_mine.at[1]),
+        (w_query_mine, cross_mine, w_mine.at[1]),
         (w_theirs_query, cross_theirs, w_theirs.at[1]),
     ):
         cross_query = jnp.dot(normed, wq[...], preferred_element_type=jnp.float32).astype(jnp.bfloat16)
         context, _ = attend_pairs(cross_query, kv.at[0], kv.at[1], enc_bias)
         context = jnp.concatenate(context, axis=0).T.astype(jnp.bfloat16)
         second = second + project_back(context, w_back[...])
-    result = full_norm(second, gain_cross, bias_cross)
+    result = full_norm(second, norms.at[2], norms.at[3])
     left, right = result[:, :width], result[:, width:]
     is_first = head == 0
     out_send[...] = jnp.where(is_first, right, left).astype(jnp.bfloat16)
@@ -449,10 +464,10 @@
     full = w_out_t.shape[0]
     half = rows // 2
     packed = width + 4 * (width // HD)
-    pad = ((0, 16 - sinks), (0, 0))
+    pad = ((0, 0), (0, 16 - sinks), (0, 0))
     whole = pl.BlockSpec(memory_space=pltpu.VMEM)
     smem = pl.BlockSpec(memory_space=pltpu.SMEM)
-    hbm = pl.BlockSpec(memory_space=pl.ANY)
+    hbm = pl.BlockSpec(memory_space=pltpu.HBM)
 
     def buf(*shape):
         return pltpu.VMEM(shape, jnp.bfloat16)
@@ -462,15 +477,17 @@
         functools.partial(layer_kernel, count, slots, sinks),
         out_shape=jax.ShapeDtypeStruct((rows, width), jnp.bfloat16),
         in_specs=[smem] * 3
-        + [whole] * 5
-        + [hbm] * 4
-        + [whole, hbm, whole, whole, whole, hbm, whole, whole],
+        + [hbm] * 16,
         out_specs=whole,
         scratch_shapes=[
             buf(slots, keys, width),
             buf(slots, keys, width),
             buf(rows + 128, width),
             buf(rows + 128, width),
+            buf(rows, width),
+            buf(half, width),
+            buf(full, width),
+            pltpu.VMEM((4, 1, full), jnp.float32),
             buf(3, rows, width),
             buf(slots, rows, width),
             buf(slots, packed, rows),
@@ -490,7 +507,7 @@
             buf(half, width),
             buf(half, width),
             dma((2, slots)),
-            dma((4,)),
+            dma((15,)),
             dma((3,)),
             dma((3,)),
             dma((slots,)),
@@ -503,7 +520,7 @@
             dma((8,)),
         ],
         compiler_params=pltpu.CompilerParams(
-            collective_id=0, has_side_effects=True, vmem_limit_bytes=52 * 1024 * 1024
+            collective_id=0, has_side_effects=True, vmem_limit_bytes=64 * 1024 * 1024
         ),
         cost_estimate=pl.CostEstimate(
             flops=4 * rows * keys * width * slots,
@@ -517,8 +534,7 @@
         queries,
         new_keys,
         new_values,
-        jnp.pad(sink_keys[0], pad),
-        jnp.pad(sink_values[0], pad),
+        jnp.pad(jnp.concatenate([sink_keys, sink_values], axis=0), pad),
         pool_keys,
         pool_values,
         cross_keys,

time: 117 us -> 108 us (0.923)
  local copies, waits for them, and re-layouts: 11.8 us -> 1.67 us
  other arithmetic: 0 us -> 1.33 us
    unnamed x25 -> x1, local copies, waits for them, and re-layouts: 10.4 us -> 1.67 us
    pad x2 -> x0, local copies, waits for them, and re-layouts: 1.39 us -> none  [the longest x1 0.69 us: per_device(): jnp.pad(sink_keys[0], pad)]
    concatenate x0 -> x1, other arithmetic: none -> 1.33 us  [per_device(): jnp.concatenate([sink_keys, sink_values], axis=0)]
where the time goes in v1:
time: 108 us
  Pallas kernels  104 us (96%)
  local copies, waits for them, and re-layouts  1.67 us (2%)
  other arithmetic  1.33 us (1%)
    pallas_call x1, Pallas kernels, per_device(): pl.pallas_call(functools.partial(layer_kernel, count, slots, sinks), out_...  104 us

profile of v1, /device:TPU:0, one launch (start us, length us, event | category | flops | bytes accessed | tf_op | source)
XLA Modules:
  0.0 107.7 jit_solution(17515860531887477976)
XLA Ops:
  0.7 1.3 %fusion.2.sink_pair = bf16[2,16,512]{2,1,0:T(8,128)(2,1)} fusion(bf16[1,4,512]{2,1,0:T(4,128)(2,1)} %param.24, bf16[1,4,512]{2,1,0:T(4,128)(2,1)} %param.23), kind=kLoop, calls=%fused_computation.3 | loop fusion | flops 114688 | bytes 40960 | tf_op jit(solution)/shard_map/concatenate | solution.py:537
  2.0 104.0 %shard_map.190 = bf16[256,512]{1,0:T(8,128)(2,1)} custom-call(s32[16,9]{1,0:T(8,128)} %block_ids.1, s32[16]{0:T(128)} %cache_lengths.1, s32[1]{0:T(128)S(6)} %copy.22.enc_lengths, bf16[256,512]{1,0:T(8,128)(2,1)} %queries.1, bf16[256,512]{1,0:T(8,128)(2,1)} %new_keys.1, bf16[256,512]{1,0:T(8,128)(2,1)} %new_values.1, bf16[2,16,512]{2,1,0:T(8,128)(2,1)} %fusion.2.sink_pair, ...), custom_call_target="tpu_custom_call" | custom-call | flops 2415919104 | bytes 9437184 | tf_op jit(solution)/shard_map/pallas_call | solution.py:476
  106.0 1.7 %copy.23 = bf16[256,512]{1,0:T(8,128)(2,1)} copy(bf16[256,512]{1,0:T(8,128)(2,1)} %shard_map.190) | data formatting | bytes 524288
